TPU v7x, 768 devices: a whole 4x8x12 slice. The times are simulated.
768 devices in a mesh: gx: 48 (over z, x), gy: 16 (over y, core).
Axes of the slice: x: 4, y: 8, z: 12, core: 2. Of those that a mesh axis runs over, the one named last changes fastest.
Arguments:
- rhs: float32 [384, 1536, 64], P('gx', 'gy'), may hold values from -6 to 6
- active: int32 [384, 1536], P('gx', 'gy'), may hold values 0 or 1
- fine_types: int32 [5, 384, 1536], P(None, 'gx', 'gy'), may hold values from 0 to 3
- fine_scales: float32 [5, 384, 1536], P(None, 'gx', 'gy'), may hold values from 0.5 to 2
- fine_table: float32 [5, 4, 64, 64], replicated, may hold values from -0.9 to 2.6
- fine_smoother: float32 [4, 64, 64], replicated, may hold values from -0.15 to 0.65
- fine_groups: int32 [384, 1536], P('gx', 'gy'), may hold values from 0 to 191
- coarse_types: int32 [5, 192, 768], P(None, 'gx', 'gy'), may hold values from 0 to 3
- coarse_scales: float32 [5, 192, 768], P(None, 'gx', 'gy'), may hold values from 0.5 to 2
- coarse_table: float32 [5, 4, 64, 64], replicated, may hold values from -3.6 to 10.4
- coarse_smoother: float32 [4, 64, 64], replicated, may hold values from -0.04 to 0.165
- coarse_groups: int32 [192, 768], P('gx', 'gy'), may hold values from 0 to 1
- coarsest: float32 [48, 2048, 2048], P('gx', 'gy'), as said below
Outputs:
- solution: float32 [384, 1536, 64], P('gx', 'gy')
- residual: float32 [384, 1536, 64], P('gx', 'gy')
Inputs may be any that keep to these rules, and one draw needn't show every extreme that they name: `coarsest`: each subgroup's matrix is symmetric. `fine_groups`: numbered row-major within the same device's tile of 4 x 48 second-level rows. `coarse_groups`: numbered within the same device's 2 third-level rows.
All inputs are finite; a program needn't handle non-finite values. No bound on the sum of `active` on one device may be relied on, other than what follows from the above.
Results may differ from a plain program's by a relative error of at most 0.00016.
Values sent between devices are 32-bit elements; how exact they have to be, the bound alone decides.
A program may use at most 64 MiB of HBM per device.

v0:
```python
import functools

import jax
import jax.numpy as jnp
from jax import lax
from jax.experimental import pallas as pl
from jax.experimental.pallas import tpu as pltpu
from jax.sharding import PartitionSpec as P

MESH = pl.DeviceIdType.MESH
F32 = jnp.float32
BF16 = jnp.bfloat16
OMEGA = 0.7

TOP = 3
ROWS = 14


def lanes_of(shape):
    return lax.broadcasted_iota(jnp.int32, shape, len(shape) - 1)


def roll(x, shift):
    shift = shift % x.shape[-1]
    return x if shift == 0 else pltpu.roll(x, shift, x.ndim - 1)


def halves(x):
    high = x.astype(BF16)
    low = (x - high.astype(F32)).astype(BF16)
    return jnp.concatenate([high, low], axis=0)


def dot(a, b):
    return jnp.dot(a, b, preferred_element_type=F32)


def pick(products, kind, scale):
    width = products.shape[1]
    y = products.reshape(4, 8, 8, width)
    kind = jnp.broadcast_to(kind[None], (8, 8, width))
    out = jnp.where(kind == 1.0, y[1], y[0])
    out = jnp.where(kind == 2.0, y[2], out)
    out = jnp.where(kind == 3.0, y[3], out)
    return (out * scale[None]).reshape(64, width)


def kernel(
    ngx, ngy,
    rhs_ref, active_ref, ftypes_ref, fscales_ref, ftab_ref, fsm_ref, fgroups_ref,
    ctypes_ref, cscales_ref, ctab_ref, csm_ref, cgroups_ref, coarsest_ref,
    sol_ref, res_ref,
    st, xa, xb, rhs_s, meta, gplane, tb, sb, c0b, fb, cplane, ctb, csb, cc0,
    ft, fs, ct, cs, member, lv, ff, m_s,
    e0_row, e0_col, e3_row, e3_col, e6_row, e6_col, ba_meta_row, ba_meta_col, ba_rhs_col, ba_rhs_row, ba_cg,
    e1_row, e1_col, rs_own, rs_up, rs_dn,
    pack_st, pack_rhs, pack_mrow, pack_mcol, cpack, parts, asm, onehot,
    load_sem, s0, r0, sb_sem, rb_sem, s1, r1, srs, rrs, rrsx, s3, r3, s6, r6, dis,
):
    gx = lax.axis_index("gx")
    gy = lax.axis_index("gy")
    up = (lax.rem(gx + ngx - 1, ngx), gy)
    down = (lax.rem(gx + 1, ngx), gy)
    left = (gx, lax.rem(gy + ngy - 1, ngy))
    right = (gx, lax.rem(gy + 1, ngy))
    has_up, has_down = gx > 0, gx < ngx - 1
    has_left, has_right = gy > 0, gy < ngy - 1

    barrier = pltpu.get_barrier_semaphore()
    for to in (up, down, left, right):
        pl.semaphore_signal(barrier, inc=1, device_id=to, device_id_type=MESH)

    load = pltpu.make_async_copy(coarsest_ref.at[0], m_s, load_sem)
    load.start()

    def send(src, dst, ssem, rsem, to):
        copy = pltpu.make_async_remote_copy(
            src_ref=src, dst_ref=dst, send_sem=ssem, recv_sem=rsem, device_id=to, device_id_type=MESH
        )
        copy.start()
        return copy

    def keep(flag, x):
        return jnp.where(flag, x, jnp.zeros_like(x))

    lane = lanes_of((64, 128))

    st[...] = jnp.zeros_like(st)
    xa[...] = jnp.zeros_like(xa)
    xb[...] = jnp.zeros_like(xb)
    rhs_s[...] = jnp.zeros_like(rhs_s)
    meta[...] = jnp.zeros_like(meta)
    gplane[...] = jnp.full_like(gplane, -1)
    cplane[...] = jnp.zeros_like(cplane)
    for i in range(8):
        rhs_s[TOP + i, :, 0:96] = rhs_ref[i]
    for d in range(5):
        meta[d, TOP:TOP + 8, 0:96] = ftypes_ref[d].astype(F32)
        meta[5 + d, TOP:TOP + 8, 0:96] = fscales_ref[d]
        cplane[d, 0:4, 0:48] = ctypes_ref[d].astype(F32)
        cplane[5 + d, 0:4, 0:48] = cscales_ref[d]
    meta[10, TOP:TOP + 8, 0:96] = active_ref[...].astype(F32)
    g = fgroups_ref[...]
    step = lambda k: (g >= 48 * k).astype(jnp.int32)
    gplane[0:8, 0:96] = g + 16 * (step(1) + step(2) + step(3))
    cplane[10, 0:4, 0:48] = (cgroups_ref[...] + 1).astype(F32)

    def split_table(block):
        high = block.astype(BF16).astype(F32)
        low = block - high
        return jnp.concatenate([high, high, low, low], axis=1).astype(BF16)

    fs[...] = split_table(fsm_ref[...].reshape(256, 64))
    cs[...] = split_table(csm_ref[...].reshape(256, 64))
    for d in range(5):
        ft[d] = split_table(ftab_ref[d].reshape(256, 64))
        ct[d] = split_table(ctab_ref[d].reshape(256, 64))

    def weights(rows):
        for a in rows:
            for d in range(5):
                shift = {3: -1, 4: 1}.get(d, 0)
                tb[d, a] = jnp.broadcast_to(roll(meta[d, a:a + 1, :], shift), (8, 128))
                sb[d, a] = jnp.broadcast_to(roll(meta[5 + d, a:a + 1, :], shift), (8, 128))
            scale = meta[5, a:a + 1, :]
            inside = meta[10, a:a + 1, :]
            factor = jnp.where(scale > 0.0, OMEGA * inside / jnp.where(scale > 0.0, scale, 1.0), 0.0)
            c0b[a] = jnp.broadcast_to(factor, (8, 128))
            fb[a] = jnp.broadcast_to(inside, (8, 128))

    weights(range(TOP, TOP + 8))

    def both(ref, a):
        return jnp.concatenate([ref[a], ref[a + 1]], axis=-1)

    def rhs_operand(x, a):
        pair = both(x, a)
        return jnp.concatenate([pair, pair], axis=0)

    def apply_pair(x, a):
        kinds = lambda d: jnp.concatenate([tb[d, a], tb[d, a + 1]], axis=-1)
        scales = lambda d: jnp.concatenate([sb[d, a], sb[d, a + 1]], axis=-1)
        here = rhs_operand(x, a)
        out = pick(dot(ft[0], here), kinds(0), scales(0))
        out = out + pick(dot(ft[1], rhs_operand(x, a - 1)), kinds(1), scales(1))
        out = out + pick(dot(ft[2], rhs_operand(x, a + 1)), kinds(2), scales(2))
        for d, shift in ((3, 1), (4, -1)):
            part = pick(dot(ft[d], here), kinds(d), scales(d))
            out = out + jnp.concatenate([roll(part[:, :128], shift), roll(part[:, 128:], shift)], axis=-1)
        return out

    def smooth_pair(r, a):
        parts2 = halves(r)
        y = dot(fs[...], jnp.concatenate([parts2, parts2], axis=0))
        kind = jnp.concatenate([tb[0, a], tb[0, a + 1]], axis=-1)
        factor = jnp.concatenate([c0b[a], c0b[a + 1]], axis=-1)
        return pick(y, kind, factor)

    def put(x, a, value):
        x[a] = halves(value)

    def smooth_rows(source, target, first, pairs):
        def body(k, carry):
            a = first + 2 * k
            r = both(rhs_s, a) - apply_pair(source, a)
            new = both(st, a) + smooth_pair(r, a)
            for n in range(2):
                part = new[:, 128 * n:128 * n + 128]
                st[a + n] = part
                put(target, a + n, part)
            return carry
        lax.fori_loop(0, pairs, body, 0)

    def level_rows(source):
        def body(k, carry):
            a = TOP + 2 * k
            inside = jnp.concatenate([fb[a], fb[a + 1]], axis=-1)
            r = (both(rhs_s, a) - apply_pair(source, a)).reshape(8, 8, 256) * inside[None]
            lv[k] = halves(r.reshape(64, 256))
            return carry
        lax.fori_loop(0, 4, body, 0)

    def first_body(k, carry):
        a = TOP + 2 * k
        new = smooth_pair(both(rhs_s, a), a)
        for n in range(2):
            part = new[:, 128 * n:128 * n + 128]
            st[a + n] = part
            put(xa, a + n, part)
        return carry

    lax.fori_loop(0, 4, first_body, 0)

    def pack_columns(field, slot, out):
        first = jnp.zeros((64, 128), F32)
        last = jnp.zeros((64, 128), F32)
        for i in range(8):
            block = field[TOP + i]
            mask = (lane >= 4 * i) & (lane < 4 * i + 3)
            first = jnp.where(mask, roll(block, 4 * i), first)
            last = jnp.where(mask, roll(block, 4 * i - 93), last)
        out[slot] = first
        out[slot + 1] = last

    def with_columns(block, from_left, from_right, i):
        block = jnp.where((lane >= 96) & (lane < 99), roll(from_right, 96 - 4 * i), block)
        return jnp.where(lane >= 125, roll(from_left, 125 - 4 * i), block)

    pack_columns(st, 0, pack_st)
    pl.semaphore_wait(barrier, 4)
    e0 = [
        send(st.at[TOP], e0_row.at[1], s0.at[0], r0.at[1], up),
        send(st.at[TOP + 7], e0_row.at[0], s0.at[1], r0.at[0], down),
        send(pack_st.at[0], e0_col.at[1], s0.at[2], r0.at[3], left),
        send(pack_st.at[1], e0_col.at[0], s0.at[3], r0.at[2], right),
    ]

    row256 = lax.broadcasted_iota(jnp.int32, (256, 128), 0)
    for i in range(8):
        code = jnp.broadcast_to(gplane[i:i + 1, :], (256, 128))
        member[:, 128 * i:128 * i + 128] = jnp.where(row256 == code, 1.0, 0.0).astype(BF16)

    cweights = []
    for k in range(11):
        plane = cplane[k]
        low = plane[0:1, :] + roll(plane[1:2, :], 64)
        high = plane[2:3, :] + roll(plane[3:4, :], 64)
        cweights.append((low, high))
    for d in range(5):
        shift = {3: -1, 4: 1}.get(d, 0)
        for n in range(2):
            ctb[d, :, 128 * n:128 * n + 128] = jnp.broadcast_to(roll(cweights[d][n], shift), (8, 128))
            csb[d, :, 128 * n:128 * n + 128] = jnp.broadcast_to(roll(cweights[5 + d][n], shift), (8, 128))
    for n in range(2):
        scale = cweights[5][n]
        factor = jnp.where(scale > 0.0, OMEGA / jnp.where(scale > 0.0, scale, 1.0), 0.0)
        cc0[:, 128 * n:128 * n + 128] = jnp.broadcast_to(factor, (8, 128))
    cpack[...] = jnp.concatenate([cweights[10][0], cweights[10][1], jnp.zeros((6, 128), F32)], axis=0)

    for k in range(11):
        pack_mrow[0, 2 * k:2 * k + 2, :] = meta[k, TOP:TOP + 2, :]
        pack_mrow[1, 2 * k:2 * k + 2, :] = meta[k, TOP + 6:TOP + 8, :]
    pack_mrow[0, 22:24, :] = jnp.zeros((2, 128), F32)
    pack_mrow[1, 22:24, :] = jnp.zeros((2, 128), F32)
    lane8 = lanes_of((8, 128))
    first = jnp.zeros((8, 128), F32)
    last = jnp.zeros((8, 128), F32)
    for k in range(11):
        block = meta[k, TOP:TOP + 8, :]
        mask = (lane8 >= 2 * k) & (lane8 < 2 * k + 2)
        first = jnp.where(mask, roll(block, 2 * k), first)
        last = jnp.where(mask, roll(block, 2 * k - 94), last)
    pack_mcol[0] = first
    pack_mcol[1] = last
    pack_columns(rhs_s, 0, pack_rhs)

    for copy in e0:
        copy.wait_recv()
    put(xa, TOP - 1, keep(has_up, e0_row[0]))
    put(xa, TOP + 8, keep(has_down, e0_row[1]))
    from_left = keep(has_left, e0_col[0])
    from_right = keep(has_right, e0_col[1])
    for i in range(8):
        put(xa, TOP + i, with_columns(st[TOP + i], from_left, from_right, i))
    for k, hop in enumerate((2, -2)):
        pl.semaphore_signal(dis.at[0], inc=1, device_id=(gx, lax.rem(gy + ngy + hop, ngy)), device_id_type=MESH)

    low_half = lane < 64

    def coarse_operands(c0, c1, top, bottom):
        swapped0, swapped1 = roll(c0, 64), roll(c1, 64)
        middle = jnp.where(low_half, swapped0, swapped1)
        before0 = jnp.where(low_half, top, swapped0)
        after1 = jnp.where(low_half, swapped1, bottom)
        def operand(p, q):
            h = halves(jnp.concatenate([p, q], axis=1))
            return jnp.concatenate([h, h], axis=0)
        return operand(c0, c1), operand(before0, middle), operand(middle, after1)

    def coarse_apply(c0, c1, top, bottom):
        here, before, after = coarse_operands(c0, c1, top, bottom)
        out = pick(dot(ct[0], here), ctb[0], csb[0])
        out = out + pick(dot(ct[1], before), ctb[1], csb[1])
        out = out + pick(dot(ct[2], after), ctb[2], csb[2])
        for d, shift in ((3, 1), (4, -1)):
            part = pick(dot(ct[d], here), ctb[d], csb[d])
            out = out + jnp.concatenate([roll(part[:, :128], shift), roll(part[:, 128:], shift)], axis=-1)
        return out

    def coarse_smooth(r):
        h = halves(r)
        return pick(dot(cs[...], jnp.concatenate([h, h], axis=0)), ctb[0], cc0)

    left_lanes = (lane == 127) | (lane == 63)
    right_lanes = (lane == 48) | (lane == 112)

    def background():
        copies = [
            send(rhs_s.at[pl.ds(TOP, 2)], ba_rhs_row.at[1], sb_sem.at[0], rb_sem.at[0], up),
            send(rhs_s.at[pl.ds(TOP + 6, 2)], ba_rhs_row.at[0], sb_sem.at[1], rb_sem.at[1], down),
            send(pack_mrow.at[0], ba_meta_row.at[1], sb_sem.at[2], rb_sem.at[2], up),
            send(pack_mrow.at[1], ba_meta_row.at[0], sb_sem.at[3], rb_sem.at[3], down),
        ]
        slot = 4
        for k, x in enumerate((gx, up[0], down[0])):
            for side, to in ((0, left[1]), (1, right[1])):
                copies.append(send(pack_mcol.at[side], ba_meta_col.at[k, side], sb_sem.at[slot], rb_sem.at[slot], (x, to)))
                copies.append(
                    send(pack_rhs.at[side], ba_rhs_col.at[k, side], sb_sem.at[slot + 1], rb_sem.at[slot + 1], (x, to))
                )
                slot += 2
        for k, to in enumerate((down, up, right, left)):
            copies.append(send(cpack, ba_cg.at[k], sb_sem.at[slot + k], rb_sem.at[slot + k], to))
        return copies

    def disseminate(level, hop):
        pl.semaphore_wait(dis.at[level], 2)
        if hop:
            for h in (hop, -hop):
                pl.semaphore_signal(
                    dis.at[level + 1], inc=1, device_id=(gx, lax.rem(gy + ngy + h, ngy)), device_id_type=MESH
                )

    def unpack_groups():
        lane1 = lanes_of((1, 128))
        is_left = (lane1 == 127) | (lane1 == 63)
        is_right = (lane1 == 48) | (lane1 == 112)
        codes = []
        for n in range(2):
            own = cpack[n:n + 1, :]
            code = jnp.where(own > 0.0, 8.0 * (own - 1.0), -1.0)
            fl = roll(ba_cg[2, n:n + 1, :], 80)
            fr = roll(ba_cg[3, n:n + 1, :], 48)
            code = jnp.where(is_left & has_left, 8.0 * (fl - 1.0) + 1.0, code)
            code = jnp.where(is_right & has_right, 8.0 * (fr - 1.0) + 2.0, code)
            codes.append(code)
        top = roll(ba_cg[0, 1:2, :], 64)
        bottom = roll(ba_cg[1, 0:1, :], 64)
        ends = jnp.full((1, 128), -1.0, F32)
        ends = jnp.where((lane1 < 48) & has_up, 8.0 * (top - 1.0) + 3.0, ends)
        ends = jnp.where((lane1 >= 64) & (lane1 < 112) & has_down, 8.0 * (bottom - 1.0) + 4.0, ends)
        codes.append(ends)
        rows = lax.broadcasted_iota(jnp.int32, (128, 128), 0)
        entry = jnp.where(rows < 32, lax.rem(rows, 16), 99).astype(F32)
        for n in range(3):
            hit = entry == jnp.broadcast_to(codes[n], (128, 128))
            onehot[:, 128 * n:128 * n + 128] = jnp.where(hit, 1.0, 0.0).astype(BF16)

    def unpack_halo():
        lane16 = lanes_of((16, 128))
        flags = ((has_left, has_right), (has_up, has_down))
        asm[...] = jnp.zeros_like(asm)
        for side in range(2):
            asm[side, 3:11, :] = ba_meta_col[0, side]
            asm[side, 1:3, :] = ba_meta_col[2, side, 6:8, :]
            asm[side, 11:13, :] = ba_meta_col[1, side, 0:2, :]
        for k in range(11):
            for rows, side, flag in ((slice(1, 3), 0, has_up), (slice(11, 13), 1, has_down)):
                block = ba_meta_row[side, 2 * k:2 * k + 2, :]
                meta[k, rows, :] = keep(flag, block) if k == 10 else block
            block = meta[k]
            fr = roll(asm[0], 96 - 2 * k)
            fl = roll(asm[1], 126 - 2 * k)
            if k == 10:
                fr, fl = keep(has_right, fr), keep(has_left, fl)
                row = lax.broadcasted_iota(jnp.int32, (16, 128), 0)
                dead = ((row < 3) & jnp.logical_not(has_up)) | ((row > 10) & jnp.logical_not(has_down))
                fr, fl = jnp.where(dead, 0.0, fr), jnp.where(dead, 0.0, fl)
            block = jnp.where((lane16 >= 96) & (lane16 < 98), fr, block)
            meta[k] = jnp.where(lane16 >= 126, fl, block)
        for a in range(1, 13):
            if a < 3:
                block, source, i = ba_rhs_row[0, a - 1], 2, a + 5
            elif a < 11:
                block, source, i = rhs_s[a], 0, a - 3
            else:
                block, source, i = ba_rhs_row[1, a - 11], 1, a - 11
            rhs_s[a] = with_columns(block, ba_rhs_col[source, 1], ba_rhs_col[source, 0], i)
        weights(range(1, 13))

    behind = []
    e1_sent = []

    def taken(count, rows, sem):
        shape = rs_own.at[0, pl.ds(0, count), pl.ds(0, rows)]
        pltpu.make_async_copy(shape, shape, sem).wait()

    def correct(cycle):
        summed = jnp.zeros((128, 256), F32)
        for k in range(4):
            summed = summed + lax.dot_general(
                lv[k], member[:, 256 * k:256 * k + 256], (((1,), (1,)), ((), ())), preferred_element_type=F32
            )
        first_rhs = summed[:64] + summed[64:]
        fix = coarse_smooth(first_rhs)
        f0, f1 = fix[:, :128], fix[:, 128:]
        ff[cycle, 0] = f0
        ff[cycle, 1] = f1
        ff[cycle, 2] = jnp.where(
            (lane == 0) | (lane == 64), f0, jnp.where((lane == 1) | (lane == 65), roll(f1, 1), 0.0)
        )
        ff[cycle, 3] = jnp.where(
            (lane == 47) | (lane == 111), f0, jnp.where((lane == 48) | (lane == 112), roll(f1, 1), 0.0)
        )
        e1 = [
            send(ff.at[cycle, 0], e1_row.at[cycle, 1], s1.at[cycle, 0], r1.at[cycle, 1], up),
            send(ff.at[cycle, 1], e1_row.at[cycle, 0], s1.at[cycle, 1], r1.at[cycle, 0], down),
            send(ff.at[cycle, 2], e1_col.at[cycle, 1], s1.at[cycle, 2], r1.at[cycle, 3], left),
            send(ff.at[cycle, 3], e1_col.at[cycle, 0], s1.at[cycle, 3], r1.at[cycle, 2], right),
        ]
        e1_sent.extend(e1)
        if cycle == 0:
            behind.extend(background())
            disseminate(0, 4)
            disseminate(1, 1)
        for copy in e1:
            copy.wait_recv()
        top = roll(keep(has_up, e1_row[cycle, 0]), 64)
        bottom = roll(keep(has_down, e1_row[cycle, 1]), 64)
        fl = keep(has_left, e1_col[cycle, 0])
        fr = keep(has_right, e1_col[cycle, 1])
        h0 = jnp.where(left_lanes, roll(fl, 80), jnp.where(right_lanes, roll(fr, 48), f0))
        h1 = jnp.where(left_lanes, roll(fl, 79), jnp.where(right_lanes, roll(fr, 47), f1))
        leftover = first_rhs - coarse_apply(h0, h1, top, bottom)
        l0, l1 = leftover[:, :128], leftover[:, 128:]
        entries = []
        for h in range(2):
            m0 = jnp.broadcast_to(cpack[0:1, :] == h + 1.0, (64, 128))
            m1 = jnp.broadcast_to(cpack[1:2, :] == h + 1.0, (64, 128))
            total = jnp.where(m0, l0, 0.0) + jnp.where(m1, l1, 0.0)
            entries.append(jnp.sum(total, axis=1, keepdims=True))
        column = jnp.broadcast_to(jnp.concatenate(entries, axis=0), (128, 128))
        if cycle == 0:
            load.wait()
        for q in range(ngy):
            row = jnp.sum(m_s[:, 128 * q:128 * q + 128] * column, axis=0, keepdims=True)
            parts[cycle, q, 0:1, :] = row
            if q + 1 < ngy:
                parts[cycle, q + 1, 1:2, :] = row
            if q > 0:
                parts[cycle, q - 1, 2:3, :] = row
        parts[cycle, 0, 1:2, :] = jnp.zeros((1, 128), F32)
        parts[cycle, ngy - 1, 2:3, :] = jnp.zeros((1, 128), F32)
        if cycle == 0:
            disseminate(2, 0)

        def own_copy(k):
            q = lax.rem(gy + k, ngy)
            return pltpu.make_async_remote_copy(
                src_ref=parts.at[cycle, q, pl.ds(0, 3)], dst_ref=rs_own.at[cycle, gy, pl.ds(0, 3)],
                send_sem=srs.at[cycle, 0], recv_sem=rrs.at[cycle], device_id=(gx, q), device_id_type=MESH,
            )

        def cross_copy(k, which):
            q = lax.rem(gy + k, ngy)
            to, dst = (up[0], rs_dn) if which == 0 else (down[0], rs_up)
            return pltpu.make_async_remote_copy(
                src_ref=parts.at[cycle, q, pl.ds(0, 1)], dst_ref=dst.at[cycle, gy, pl.ds(0, 1)],
                send_sem=srs.at[cycle, 1 + which], recv_sem=rrsx.at[cycle, which], device_id=(to, q), device_id_type=MESH,
            )

        for k in range(1, ngy):
            own_copy(k).start()
        for k in range(ngy):
            cross_copy(k, 0).start()
            cross_copy(k, 1).start()
        rs_own[cycle, gy, 0:3, :] = parts[cycle, gy, 0:3, :]
        if cycle == 0:
            for copy in behind:
                copy.wait()
            unpack_groups()
            unpack_halo()
        taken(ngy - 1, 3, rrs.at[cycle])
        taken(ngy, 1, rrsx.at[cycle, 0])
        taken(ngy, 1, rrsx.at[cycle, 1])
        own = rs_own[cycle, 0, 0:3, :]
        above = rs_up[cycle, 0, 0:1, :]
        below = rs_dn[cycle, 0, 0:1, :]
        for q in range(1, ngy):
            own = own + rs_own[cycle, q, 0:3, :]
            above = above + rs_up[cycle, q, 0:1, :]
            below = below + rs_dn[cycle, q, 0:1, :]
        five = jnp.concatenate([own, above, below, jnp.zeros((3, 128), F32)], axis=0)
        both_groups = jnp.concatenate([five, roll(five, 64)], axis=0)
        high = both_groups.astype(BF16).astype(F32)
        tall = jnp.concatenate([high, both_groups - high, jnp.zeros((96, 128), F32)], axis=0)
        lifted = dot(tall.T[0:64].astype(BF16), onehot[...])
        p0, p1, ends = lifted[:, :128], lifted[:, 128:256], lifted[:, 256:]
        rest = leftover - coarse_apply(p0, p1, ends, ends)
        fix = fix + lifted[:, :256] + coarse_smooth(rest)
        spread = dot(halves(fix), member[...])
        spread = spread[:64] + spread[64:]
        for i in range(8):
            block = spread[:, 128 * i:128 * i + 128].reshape(8, 8, 128) * fb[TOP + i][None]
            st[TOP + i] = st[TOP + i] + block.reshape(64, 128)

    def exchange(width, row_buf, col_buf, ssem, rsem, slot):
        pack_columns(st, slot, pack_st)
        copies = [
            send(st.at[pl.ds(TOP, width)], row_buf.at[1], ssem.at[0], rsem.at[1], up),
            send(st.at[pl.ds(TOP + 8 - width, width)], row_buf.at[0], ssem.at[1], rsem.at[0], down),
        ]
        n = 2
        for k, x in enumerate((gx, up[0], down[0])):
            for side, to in ((0, left[1]), (1, right[1])):
                copies.append(send(pack_st.at[slot + side], col_buf.at[k, side], ssem.at[n], rsem.at[n], (x, to)))
                n += 1
        for copy in copies:
            copy.wait()
        for a in range(TOP - width, TOP + 8 + width):
            if a < 3:
                block, source, i, flag = row_buf[0, a - (TOP - width)], 2, a + 5, has_up
            elif a < 11:
                block, source, i, flag = st[a], 0, a - 3, None
            else:
                block, source, i, flag = row_buf[1, a - 11], 1, a - 11, has_down
            fl = keep(has_left, col_buf[source, 1])
            fr = keep(has_right, col_buf[source, 0])
            block = with_columns(block, fl, fr, i)
            if flag is not None:
                block = keep(flag, block)
            st[a] = block
            put(xa, a, block)

    level_rows(xa)
    for copy in e0:
        copy.wait_send()
    correct(0)
    exchange(3, e3_row, e3_col, s3, r3, 2)
    smooth_rows(xa, xb, 1, 6)
    smooth_rows(xb, xa, 2, 5)
    level_rows(xa)
    correct(1)
    exchange(2, e6_row, e6_col, s6, r6, 4)
    smooth_rows(xa, xb, 2, 5)

    def final_body(k, carry):
        a = TOP + 2 * k
        inside = jnp.concatenate([fb[a], fb[a + 1]], axis=-1)
        r = (both(rhs_s, a) - apply_pair(xb, a)).reshape(8, 8, 256) * inside[None]
        r = r.reshape(64, 256)
        for n in range(2):
            res_ref[2 * k + n] = r[:, 128 * n:128 * n + 96]
            sol_ref[2 * k + n] = st[a + n][:, 0:96]
        return carry

    lax.fori_loop(0, 4, final_body, 0)

    for copy in e1_sent:
        copy.wait_send()
    for cycle in range(2):
        taken(ngy - 1, 3, srs.at[cycle, 0])
        taken(ngy, 1, srs.at[cycle, 1])
        taken(ngy, 1, srs.at[cycle, 2])


def solution(mesh):
    ngx, ngy = mesh.shape["gx"], mesh.shape["gy"]

    def shards(
        rhs, active, fine_types, fine_scales, fine_table, fine_smoother, fine_groups,
        coarse_types, coarse_scales, coarse_table, coarse_smoother, coarse_groups, coarsest,
    ):
        vmem = pl.BlockSpec(memory_space=pltpu.VMEM)
        field = jax.ShapeDtypeStruct((8, 64, 96), F32)
        dma = pltpu.SemaphoreType.DMA
        sol, res = pl.pallas_call(
            functools.partial(kernel, ngx, ngy),
            out_shape=(field, field),
            in_specs=[vmem] * 12 + [pl.BlockSpec(memory_space=pl.ANY)],
            out_specs=(vmem, vmem),
            scratch_shapes=[
                pltpu.VMEM((ROWS, 64, 128), F32),
                pltpu.VMEM((ROWS, 128, 128), BF16),
                pltpu.VMEM((ROWS, 128, 128), BF16),
                pltpu.VMEM((ROWS, 64, 128), F32),
                pltpu.VMEM((11, 16, 128), F32),
                pltpu.VMEM((8, 128), jnp.int32),
                pltpu.VMEM((5, ROWS, 8, 128), F32),
                pltpu.VMEM((5, ROWS, 8, 128), F32),
                pltpu.VMEM((ROWS, 8, 128), F32),
                pltpu.VMEM((ROWS, 8, 128), F32),
                pltpu.VMEM((11, 8, 128), F32),
                pltpu.VMEM((5, 8, 256), F32),
                pltpu.VMEM((5, 8, 256), F32),
                pltpu.VMEM((8, 256), F32),
                pltpu.VMEM((5, 256, 256), BF16),
                pltpu.VMEM((256, 256), BF16),
                pltpu.VMEM((5, 256, 256), BF16),
                pltpu.VMEM((256, 256), BF16),
                pltpu.VMEM((256, 1024), BF16),
                pltpu.VMEM((4, 128, 256), BF16),
                pltpu.VMEM((2, 4, 64, 128), F32),
                pltpu.VMEM((128, 128 * ngy), F32),
                pltpu.VMEM((2, 64, 128), F32),
                pltpu.VMEM((2, 64, 128), F32),
                pltpu.VMEM((2, 3, 64, 128), F32),
                pltpu.VMEM((3, 2, 64, 128), F32),
                pltpu.VMEM((2, 2, 64, 128), F32),
                pltpu.VMEM((3, 2, 64, 128), F32),
                pltpu.VMEM((2, 24, 128), F32),
                pltpu.VMEM((3, 2, 8, 128), F32),
                pltpu.VMEM((3, 2, 64, 128), F32),
                pltpu.VMEM((2, 2, 64, 128), F32),
                pltpu.VMEM((4, 8, 128), F32),
                pltpu.VMEM((2, 2, 64, 128), F32),
                pltpu.VMEM((2, 2, 64, 128), F32),
                pltpu.VMEM((2, ngy, 8, 128), F32),
                pltpu.VMEM((2, ngy, 8, 128), F32),
                pltpu.VMEM((2, ngy, 8, 128), F32),
                pltpu.VMEM((6, 64, 128), F32),
                pltpu.VMEM((2, 64, 128), F32),
                pltpu.VMEM((2, 24, 128), F32),
                pltpu.VMEM((2, 8, 128), F32),
                pltpu.VMEM((8, 128), F32),
                pltpu.VMEM((2, ngy, 8, 128), F32),
                pltpu.VMEM((2, 16, 128), F32),
                pltpu.VMEM((128, 384), BF16),
                dma,
                dma((4,)), dma((4,)),
                dma((20,)), dma((20,)),
                dma((2, 4)), dma((2, 4)),
                dma((2, 3)), dma((2,)), dma((2, 2)),
                dma((8,)), dma((8,)),
                dma((8,)), dma((8,)),
                pltpu.SemaphoreType.REGULAR((3,)),
            ],
            compiler_params=pltpu.CompilerParams(
                collective_id=0, has_side_effects=True, vmem_limit_bytes=48 * 2**20
            ),
        )(
            jnp.swapaxes(rhs, 1, 2), active, fine_types, fine_scales, fine_table, fine_smoother, fine_groups,
            coarse_types, coarse_scales, coarse_table, coarse_smoother, coarse_groups, coarsest,
        )
        return jnp.swapaxes(sol, 1, 2), jnp.swapaxes(res, 1, 2)

    return jax.shard_map(
        shards,
        mesh=mesh,
        in_specs=(
            P("gx", "gy", None),
            P("gx", "gy"),
            P(None, "gx", "gy"),
            P(None, "gx", "gy"),
            P(),
            P(),
            P("gx", "gy"),
            P(None, "gx", "gy"),
            P(None, "gx", "gy"),
            P(),
            P(),
            P("gx", "gy"),
            P("gx", "gy", None),
        ),
        out_specs=(P("gx", "gy", None), P("gx", "gy", None)),
        check_vma=False,
    )
```

profile of v0, /device:TPU:1, one launch (start us, length us, event | category | flops | bytes accessed | tf_op | source)
XLA Modules:
  0.0 95.3 jit_solution(3820863978728551280)
XLA Ops:
  0.6 0.0 copy-start
  0.6 1.2 %copy-done = f32[1,128,2048]{2,1,0:T(8,128)S(1)} copy-done((f32[1,128,2048]{2,1,0:T(8,128)S(1)}, f32[1,128,2048]{2,1,0:T(8,128)}, u32[]{:S(2)}) %copy-start) | copy-done | bytes 1048600
  1.9 0.0 copy-start.1
  1.9 1.1 %copy-done.1 = f32[5,4,64,64]{3,2,1,0:T(8,128)S(1)} copy-done((f32[5,4,64,64]{3,2,1,0:T(8,128)S(1)}, f32[5,4,64,64]{3,2,1,0:T(8,128)}, u32[]{:S(2)}) %copy-start.1) | copy-done | bytes 327704
  2.9 0.0 copy-start.2
  3.0 1.1 %copy-done.2 = f32[5,4,64,64]{3,2,1,0:T(8,128)S(1)} copy-done((f32[5,4,64,64]{3,2,1,0:T(8,128)S(1)}, f32[5,4,64,64]{3,2,1,0:T(8,128)}, u32[]{:S(2)}) %copy-start.2) | copy-done | bytes 327704
  4.0 0.0 copy-start.3
  4.0 0.9 copy-done.3
  5.0 0.9 copy-done.4
  5.9 0.0 copy-start.5
  5.9 0.9 copy-done.5
  6.8 0.0 copy-start.6
  6.8 0.7 copy-done.6
  7.5 0.0 copy-start.7
  7.5 0.7 copy-done.7
  8.3 0.0 copy-start.8
  8.3 0.7 copy-done.8
  9.0 0.7 copy-done.9
  9.7 0.7 copy-done.10
  10.3 0.7 copy-done.11
  11.0 0.7 copy-done.12
  11.7 82.2 %shard_map.140 = (f32[8,64,96]{2,1,0:T(8,128)S(1)}, f32[8,64,96]{2,1,0:T(8,128)S(1)}) custom-call(f32[8,64,96]{2,1,0:T(8,128)S(1)} %bitcast.3, s32[8,96]{1,0:T(8,128)S(1)} %copy-done.10, s32[5,8,96]{2,1,0:T(8,128)S(1)} %copy-done.6, f32[5,8,96]{2,1,0:T(8,128)S(1)} %copy-done.7, f32[5,4,64,64]{3,2,1,0:T(8,128)S(1)} %copy-done.1, f32[4,64,64]{2,1,0:T(8,128)S(1)} %copy-done.4, ...), custom_call_target="tpu_custom_call" | custom-call | tf_op jit(solution)/shard_map/pallas_call | solution.py:567
  93.9 0.7 copy.17
  94.6 0.7 copy.18
  (5 shorter events, 0.0 us)
Async XLA Ops:
  0.6 1.2 %copy-start = (f32[1,128,2048]{2,1,0:T(8,128)S(1)}, f32[1,128,2048]{2,1,0:T(8,128)}, u32[]{:S(2)}) copy-start(f32[1,128,2048]{2,1,0:T(8,128)} %coarsest_ref.1) | copy-start | bytes 3145732
  1.9 1.1 %copy-start.1 = (f32[5,4,64,64]{3,2,1,0:T(8,128)S(1)}, f32[5,4,64,64]{3,2,1,0:T(8,128)}, u32[]{:S(2)}) copy-start(f32[5,4,64,64]{3,2,1,0:T(8,128)} %ftab_ref.1) | copy-start | bytes 983044
  2.9 1.1 %copy-start.2 = (f32[5,4,64,64]{3,2,1,0:T(8,128)S(1)}, f32[5,4,64,64]{3,2,1,0:T(8,128)}, u32[]{:S(2)}) copy-start(f32[5,4,64,64]{3,2,1,0:T(8,128)} %ctab_ref.1) | copy-start | bytes 983044
  4.0 0.9 copy-start.3
  5.0 0.9 copy-start.4
  5.9 0.9 copy-start.5
  6.8 0.7 copy-start.6
  7.5 0.7 copy-start.7
  8.3 0.7 copy-start.8
  9.0 0.7 copy-start.9
  9.7 0.7 copy-start.10
  10.3 0.7 copy-start.11
  11.0 0.7 copy-start.12
where the time goes:
time: 95.9 us; the launch traced here: 95.3 us
  Pallas kernels  82.2 us (86%)
  local copies, waits for them, and re-layouts  12.5 us (13%)
    pallas_call x1, Pallas kernels, shards(): pl.pallas_call(functools.partial(kernel, ngx, ngy), out_shape=(field, fie...  82.2 us
    unnamed x28, local copies, waits for them, and re-layouts  12.5 us

commit v1 on v0

--- a/solution.py
+++ b/solution.py
@@ -47,9 +47,11 @@
 
 def kernel(
     ngx, ngy,
+    rhs_in, active_in, ftypes_in, fscales_in, ftab_in, fsm_in, fgroups_in,
+    ctypes_in, cscales_in, ctab_in, csm_in, cgroups_in, coarsest_in,
+    sol_ref, res_ref,
     rhs_ref, active_ref, ftypes_ref, fscales_ref, ftab_ref, fsm_ref, fgroups_ref,
-    ctypes_ref, cscales_ref, ctab_ref, csm_ref, cgroups_ref, coarsest_ref,
-    sol_ref, res_ref,
+    ctypes_ref, cscales_ref, ctab_ref, csm_ref, cgroups_ref,
     st, xa, xb, rhs_s, meta, gplane, tb, sb, c0b, fb, cplane, ctb, csb, cc0,
     ft, fs, ct, cs, member, lv, ff, m_s,
     e0_row, e0_col, e3_row, e3_col, e6_row, e6_col, ba_meta_row, ba_meta_col, ba_rhs_col, ba_rhs_row, ba_cg,
@@ -70,8 +72,17 @@
     for to in (up, down, left, right):
         pl.semaphore_signal(barrier, inc=1, device_id=to, device_id_type=MESH)
 
-    load = pltpu.make_async_copy(coarsest_ref.at[0], m_s, load_sem)
-    load.start()
+    loads = [
+        pltpu.make_async_copy(source, target, load_sem.at[n])
+        for n, (source, target) in enumerate((
+            (rhs_in, rhs_ref), (active_in, active_ref), (ftypes_in, ftypes_ref), (fscales_in, fscales_ref),
+            (fsm_in, fsm_ref), (ftab_in, ftab_ref), (fgroups_in, fgroups_ref), (ctypes_in, ctypes_ref),
+            (cscales_in, cscales_ref), (ctab_in, ctab_ref), (csm_in, csm_ref), (cgroups_in, cgroups_ref),
+            (coarsest_in.at[0], m_s),
+        ))
+    ]
+    for copy in loads:
+        copy.start()
 
     def send(src, dst, ssem, rsem, to):
         copy = pltpu.make_async_remote_copy(
@@ -90,31 +101,20 @@
     xb[...] = jnp.zeros_like(xb)
     rhs_s[...] = jnp.zeros_like(rhs_s)
     meta[...] = jnp.zeros_like(meta)
-    gplane[...] = jnp.full_like(gplane, -1)
-    cplane[...] = jnp.zeros_like(cplane)
+    for copy in loads[:5]:
+        copy.wait()
     for i in range(8):
         rhs_s[TOP + i, :, 0:96] = rhs_ref[i]
     for d in range(5):
         meta[d, TOP:TOP + 8, 0:96] = ftypes_ref[d].astype(F32)
         meta[5 + d, TOP:TOP + 8, 0:96] = fscales_ref[d]
-        cplane[d, 0:4, 0:48] = ctypes_ref[d].astype(F32)
-        cplane[5 + d, 0:4, 0:48] = cscales_ref[d]
     meta[10, TOP:TOP + 8, 0:96] = active_ref[...].astype(F32)
-    g = fgroups_ref[...]
-    step = lambda k: (g >= 48 * k).astype(jnp.int32)
-    gplane[0:8, 0:96] = g + 16 * (step(1) + step(2) + step(3))
-    cplane[10, 0:4, 0:48] = (cgroups_ref[...] + 1).astype(F32)
-
     def split_table(block):
         high = block.astype(BF16).astype(F32)
         low = block - high
         return jnp.concatenate([high, high, low, low], axis=1).astype(BF16)
 
     fs[...] = split_table(fsm_ref[...].reshape(256, 64))
-    cs[...] = split_table(csm_ref[...].reshape(256, 64))
-    for d in range(5):
-        ft[d] = split_table(ftab_ref[d].reshape(256, 64))
-        ct[d] = split_table(ctab_ref[d].reshape(256, 64))
 
     def weights(rows):
         for a in rows:
@@ -169,7 +169,7 @@
                 st[a + n] = part
                 put(target, a + n, part)
             return carry
-        lax.fori_loop(0, pairs, body, 0)
+        lax.fori_loop(0, pairs, body, 0, unroll=True)
 
     def level_rows(source):
         def body(k, carry):
@@ -178,7 +178,7 @@
             r = (both(rhs_s, a) - apply_pair(source, a)).reshape(8, 8, 256) * inside[None]
             lv[k] = halves(r.reshape(64, 256))
             return carry
-        lax.fori_loop(0, 4, body, 0)
+        lax.fori_loop(0, 4, body, 0, unroll=True)
 
     def first_body(k, carry):
         a = TOP + 2 * k
@@ -189,7 +189,7 @@
             put(xa, a + n, part)
         return carry
 
-    lax.fori_loop(0, 4, first_body, 0)
+    lax.fori_loop(0, 4, first_body, 0, unroll=True)
 
     def pack_columns(field, slot, out):
         first = jnp.zeros((64, 128), F32)
@@ -199,8 +199,11 @@
             mask = (lane >= 4 * i) & (lane < 4 * i + 3)
             first = jnp.where(mask, roll(block, 4 * i), first)
             last = jnp.where(mask, roll(block, 4 * i - 93), last)
-        out[slot] = first
-        out[slot + 1] = last
+        for n, block in ((0, first), (1, last)):
+            out[slot + n] = sum(roll(block[16 * m:16 * m + 16], 32 * m) for m in range(4))
+
+    def unfold(block):
+        return jnp.concatenate([roll(block, -32 * m) for m in range(4)], axis=0)
 
     def with_columns(block, from_left, from_right, i):
         block = jnp.where((lane >= 96) & (lane < 99), roll(from_right, 96 - 4 * i), block)
@@ -215,6 +218,20 @@
         send(pack_st.at[1], e0_col.at[0], s0.at[3], r0.at[2], right),
     ]
 
+    for copy in loads[5:12]:
+        copy.wait()
+    cplane[...] = jnp.zeros_like(cplane)
+    gplane[...] = jnp.full_like(gplane, -1)
+    for d in range(5):
+        cplane[d, 0:4, 0:48] = ctypes_ref[d].astype(F32)
+        cplane[5 + d, 0:4, 0:48] = cscales_ref[d]
+        ft[d] = split_table(ftab_ref[d].reshape(256, 64))
+        ct[d] = split_table(ctab_ref[d].reshape(256, 64))
+    cs[...] = split_table(csm_ref[...].reshape(256, 64))
+    g = fgroups_ref[...]
+    step = lambda k: (g >= 48 * k).astype(jnp.int32)
+    gplane[0:8, 0:96] = g + 16 * (step(1) + step(2) + step(3))
+    cplane[10, 0:4, 0:48] = (cgroups_ref[...] + 1).astype(F32)
     row256 = lax.broadcasted_iota(jnp.int32, (256, 128), 0)
     for i in range(8):
         code = jnp.broadcast_to(gplane[i:i + 1, :], (256, 128))
@@ -258,8 +275,8 @@
         copy.wait_recv()
     put(xa, TOP - 1, keep(has_up, e0_row[0]))
     put(xa, TOP + 8, keep(has_down, e0_row[1]))
-    from_left = keep(has_left, e0_col[0])
-    from_right = keep(has_right, e0_col[1])
+    from_left = unfold(keep(has_left, e0_col[0]))
+    from_right = unfold(keep(has_right, e0_col[1]))
     for i in range(8):
         put(xa, TOP + i, with_columns(st[TOP + i], from_left, from_right, i))
     for k, hop in enumerate((2, -2)):
@@ -368,6 +385,7 @@
                 fr, fl = jnp.where(dead, 0.0, fr), jnp.where(dead, 0.0, fl)
             block = jnp.where((lane16 >= 96) & (lane16 < 98), fr, block)
             meta[k] = jnp.where(lane16 >= 126, fl, block)
+        rhs_cols = [[unfold(ba_rhs_col[k, side]) for side in range(2)] for k in range(3)]
         for a in range(1, 13):
             if a < 3:
                 block, source, i = ba_rhs_row[0, a - 1], 2, a + 5
@@ -375,7 +393,7 @@
                 block, source, i = rhs_s[a], 0, a - 3
             else:
                 block, source, i = ba_rhs_row[1, a - 11], 1, a - 11
-            rhs_s[a] = with_columns(block, ba_rhs_col[source, 1], ba_rhs_col[source, 0], i)
+            rhs_s[a] = with_columns(block, rhs_cols[source][1], rhs_cols[source][0], i)
         weights(range(1, 13))
 
     behind = []
@@ -431,7 +449,7 @@
             entries.append(jnp.sum(total, axis=1, keepdims=True))
         column = jnp.broadcast_to(jnp.concatenate(entries, axis=0), (128, 128))
         if cycle == 0:
-            load.wait()
+            loads[12].wait()
         for q in range(ngy):
             row = jnp.sum(m_s[:, 128 * q:128 * q + 128] * column, axis=0, keepdims=True)
             parts[cycle, q, 0:1, :] = row
@@ -459,9 +477,9 @@
                 send_sem=srs.at[cycle, 1 + which], recv_sem=rrsx.at[cycle, which], device_id=(to, q), device_id_type=MESH,
             )
 
-        for k in range(1, ngy):
-            own_copy(k).start()
-        for k in range(ngy):
+        for k in sorted(range(ngy), key=lambda k: -min(k, ngy - k)):
+            if k > 0:
+                own_copy(k).start()
             cross_copy(k, 0).start()
             cross_copy(k, 1).start()
         rs_own[cycle, gy, 0:3, :] = parts[cycle, gy, 0:3, :]
@@ -496,17 +514,22 @@
 
     def exchange(width, row_buf, col_buf, ssem, rsem, slot):
         pack_columns(st, slot, pack_st)
-        copies = [
-            send(st.at[pl.ds(TOP, width)], row_buf.at[1], ssem.at[0], rsem.at[1], up),
-            send(st.at[pl.ds(TOP + 8 - width, width)], row_buf.at[0], ssem.at[1], rsem.at[0], down),
-        ]
+        copies = []
         n = 2
-        for k, x in enumerate((gx, up[0], down[0])):
+        for k, x in ((1, up[0]), (2, down[0])):
             for side, to in ((0, left[1]), (1, right[1])):
                 copies.append(send(pack_st.at[slot + side], col_buf.at[k, side], ssem.at[n], rsem.at[n], (x, to)))
                 n += 1
+        copies.append(send(st.at[pl.ds(TOP, width)], row_buf.at[1], ssem.at[0], rsem.at[1], up))
+        copies.append(send(st.at[pl.ds(TOP + 8 - width, width)], row_buf.at[0], ssem.at[1], rsem.at[0], down))
+        for side, to in ((0, left), (1, right)):
+            copies.append(send(pack_st.at[slot + side], col_buf.at[0, side], ssem.at[n], rsem.at[n], to))
+            n += 1
         for copy in copies:
             copy.wait()
+        cols = [
+            [unfold(keep(flag, col_buf[k, side])) for side, flag in ((0, has_right), (1, has_left))] for k in range(3)
+        ]
         for a in range(TOP - width, TOP + 8 + width):
             if a < 3:
                 block, source, i, flag = row_buf[0, a - (TOP - width)], 2, a + 5, has_up
@@ -514,9 +537,7 @@
                 block, source, i, flag = st[a], 0, a - 3, None
             else:
                 block, source, i, flag = row_buf[1, a - 11], 1, a - 11, has_down
-            fl = keep(has_left, col_buf[source, 1])
-            fr = keep(has_right, col_buf[source, 0])
-            block = with_columns(block, fl, fr, i)
+            block = with_columns(block, cols[source][1], cols[source][0], i)
             if flag is not None:
                 block = keep(flag, block)
             st[a] = block
@@ -544,7 +565,7 @@
             sol_ref[2 * k + n] = st[a + n][:, 0:96]
         return carry
 
-    lax.fori_loop(0, 4, final_body, 0)
+    lax.fori_loop(0, 4, final_body, 0, unroll=True)
 
     for copy in e1_sent:
         copy.wait_send()
@@ -562,14 +583,25 @@
         coarse_types, coarse_scales, coarse_table, coarse_smoother, coarse_groups, coarsest,
     ):
         vmem = pl.BlockSpec(memory_space=pltpu.VMEM)
-        field = jax.ShapeDtypeStruct((8, 64, 96), F32)
         dma = pltpu.SemaphoreType.DMA
         sol, res = pl.pallas_call(
             functools.partial(kernel, ngx, ngy),
-            out_shape=(field, field),
-            in_specs=[vmem] * 12 + [pl.BlockSpec(memory_space=pl.ANY)],
+            out_shape=(pltpu.VMEM((8, 64, 96), F32),) * 2,
+            in_specs=[pl.BlockSpec(memory_space=pltpu.HBM)] * 13,
             out_specs=(vmem, vmem),
             scratch_shapes=[
+                pltpu.VMEM((8, 64, 96), F32),
+                pltpu.VMEM((8, 96), jnp.int32),
+                pltpu.VMEM((5, 8, 96), jnp.int32),
+                pltpu.VMEM((5, 8, 96), F32),
+                pltpu.VMEM((5, 4, 64, 64), F32),
+                pltpu.VMEM((4, 64, 64), F32),
+                pltpu.VMEM((8, 96), jnp.int32),
+                pltpu.VMEM((5, 4, 48), jnp.int32),
+                pltpu.VMEM((5, 4, 48), F32),
+                pltpu.VMEM((5, 4, 64, 64), F32),
+                pltpu.VMEM((4, 64, 64), F32),
+                pltpu.VMEM((4, 48), jnp.int32),
                 pltpu.VMEM((ROWS, 64, 128), F32),
                 pltpu.VMEM((ROWS, 128, 128), BF16),
                 pltpu.VMEM((ROWS, 128, 128), BF16),
@@ -593,14 +625,14 @@
                 pltpu.VMEM((2, 4, 64, 128), F32),
                 pltpu.VMEM((128, 128 * ngy), F32),
                 pltpu.VMEM((2, 64, 128), F32),
-                pltpu.VMEM((2, 64, 128), F32),
+                pltpu.VMEM((2, 16, 128), F32),
                 pltpu.VMEM((2, 3, 64, 128), F32),
-                pltpu.VMEM((3, 2, 64, 128), F32),
+                pltpu.VMEM((3, 2, 16, 128), F32),
                 pltpu.VMEM((2, 2, 64, 128), F32),
-                pltpu.VMEM((3, 2, 64, 128), F32),
+                pltpu.VMEM((3, 2, 16, 128), F32),
                 pltpu.VMEM((2, 24, 128), F32),
                 pltpu.VMEM((3, 2, 8, 128), F32),
-                pltpu.VMEM((3, 2, 64, 128), F32),
+                pltpu.VMEM((3, 2, 16, 128), F32),
                 pltpu.VMEM((2, 2, 64, 128), F32),
                 pltpu.VMEM((4, 8, 128), F32),
                 pltpu.VMEM((2, 2, 64, 128), F32),
@@ -608,15 +640,15 @@
                 pltpu.VMEM((2, ngy, 8, 128), F32),
                 pltpu.VMEM((2, ngy, 8, 128), F32),
                 pltpu.VMEM((2, ngy, 8, 128), F32),
-                pltpu.VMEM((6, 64, 128), F32),
-                pltpu.VMEM((2, 64, 128), F32),
+                pltpu.VMEM((6, 16, 128), F32),
+                pltpu.VMEM((2, 16, 128), F32),
                 pltpu.VMEM((2, 24, 128), F32),
                 pltpu.VMEM((2, 8, 128), F32),
                 pltpu.VMEM((8, 128), F32),
                 pltpu.VMEM((2, ngy, 8, 128), F32),
                 pltpu.VMEM((2, 16, 128), F32),
                 pltpu.VMEM((128, 384), BF16),
-                dma,
+                dma((13,)),
                 dma((4,)), dma((4,)),
                 dma((20,)), dma((20,)),
                 dma((2, 4)), dma((2, 4)),
@@ -626,7 +658,7 @@
                 pltpu.SemaphoreType.REGULAR((3,)),
             ],
             compiler_params=pltpu.CompilerParams(
-                collective_id=0, has_side_effects=True, vmem_limit_bytes=48 * 2**20
+                collective_id=0, has_side_effects=True, vmem_limit_bytes=60 * 2**20
             ),
         )(
             jnp.swapaxes(rhs, 1, 2), active, fine_types, fine_scales, fine_table, fine_smoother, fine_groups,

time: 95.9 us -> 74.6 us (0.78)
  local copies, waits for them, and re-layouts: 12.5 us -> 1.41 us
  Pallas kernels: 82.2 us -> 72.4 us
    unnamed x28 -> x2, local copies, waits for them, and re-layouts: 12.5 us -> 1.41 us
    pallas_call x1, Pallas kernels: 82.2 us -> 72.4 us  [shards(): pl.pallas_call(functools.partial(kernel, ngx, ngy), out_shape=(pltpu.VMEM...]
where the time goes in v1:
time: 74.6 us; the launch traced here: 74.4 us
  Pallas kernels  72.4 us (97%)
  local copies, waits for them, and re-layouts  1.41 us (2%)
    pallas_call x1, Pallas kernels, shards(): pl.pallas_call(functools.partial(kernel, ngx, ngy), out_shape=(pltpu.VMEM...  72.4 us

profile of v1, /device:TPU:1, one launch (start us, length us, event | category | flops | bytes accessed | tf_op | source)
XLA Modules:
  0.0 74.4 jit_solution(7671437987848071851)
XLA Ops:
  0.6 72.4 %shard_map.140 = (f32[8,64,96]{2,1,0:T(8,128)S(1)}, f32[8,64,96]{2,1,0:T(8,128)S(1)}) custom-call(f32[8,64,96]{2,1,0:T(8,128)} %bitcast.5, s32[8,96]{1,0:T(8,128)} %active_in.1, s32[5,8,96]{2,1,0:T(8,128)} %ftypes_in.1, f32[5,8,96]{2,1,0:T(8,128)} %fscales_in.1, f32[5,4,64,64]{3,2,1,0:T(8,128)} %ftab_in.1, f32[4,64,64]{2,1,0:T(8,128)} %fsm_in.1, ...), custom_call_target="tpu_custom_call" | custom-call | tf_op jit(solution)/shard_map/pallas_call | solution.py:587
  73.0 0.7 copy.17
  73.7 0.7 copy.18

commit v2 on v1

--- a/solution.py
+++ b/solution.py
@@ -137,17 +137,22 @@
         pair = both(x, a)
         return jnp.concatenate([pair, pair], axis=0)
 
-    def apply_pair(x, a):
-        kinds = lambda d: jnp.concatenate([tb[d, a], tb[d, a + 1]], axis=-1)
-        scales = lambda d: jnp.concatenate([sb[d, a], sb[d, a + 1]], axis=-1)
-        here = rhs_operand(x, a)
-        out = pick(dot(ft[0], here), kinds(0), scales(0))
-        out = out + pick(dot(ft[1], rhs_operand(x, a - 1)), kinds(1), scales(1))
-        out = out + pick(dot(ft[2], rhs_operand(x, a + 1)), kinds(2), scales(2))
-        for d, shift in ((3, 1), (4, -1)):
-            part = pick(dot(ft[d], here), kinds(d), scales(d))
-            out = out + jnp.concatenate([roll(part[:, :128], shift), roll(part[:, 128:], shift)], axis=-1)
-        return out
+    def apply_rows(x, first, pairs, consume):
+        before = dot(ft[1024:1280], rhs_operand(x, first - 1))
+        for k in range(pairs):
+            a = first + 2 * k
+            kinds = lambda d: jnp.concatenate([tb[d, a], tb[d, a + 1]], axis=-1)
+            scales = lambda d: jnp.concatenate([sb[d, a], sb[d, a + 1]], axis=-1)
+            here = dot(ft[0:768], rhs_operand(x, a))
+            after = dot(ft[768:1024] if k == pairs - 1 else ft[768:1280], rhs_operand(x, a + 1))
+            out = pick(here[0:256], kinds(0), scales(0))
+            out = out + pick(before, kinds(1), scales(1))
+            out = out + pick(after[0:256], kinds(2), scales(2))
+            for d, shift in ((3, 1), (4, -1)):
+                part = pick(here[256 * (d - 2):256 * (d - 1)], kinds(d), scales(d))
+                out = out + jnp.concatenate([roll(part[:, :128], shift), roll(part[:, 128:], shift)], axis=-1)
+            before = after[256:]
+            consume(a, out)
 
     def smooth_pair(r, a):
         parts2 = halves(r)
@@ -160,25 +165,23 @@
         x[a] = halves(value)
 
     def smooth_rows(source, target, first, pairs):
-        def body(k, carry):
-            a = first + 2 * k
-            r = both(rhs_s, a) - apply_pair(source, a)
+        def consume(a, out):
+            r = both(rhs_s, a) - out
             new = both(st, a) + smooth_pair(r, a)
             for n in range(2):
                 part = new[:, 128 * n:128 * n + 128]
                 st[a + n] = part
                 put(target, a + n, part)
-            return carry
-        lax.fori_loop(0, pairs, body, 0, unroll=True)
-
-    def level_rows(source):
-        def body(k, carry):
-            a = TOP + 2 * k
+
+        apply_rows(source, first, pairs, consume)
+
+    def level_rows(source, first, pairs):
+        def consume(a, out):
             inside = jnp.concatenate([fb[a], fb[a + 1]], axis=-1)
-            r = (both(rhs_s, a) - apply_pair(source, a)).reshape(8, 8, 256) * inside[None]
-            lv[k] = halves(r.reshape(64, 256))
-            return carry
-        lax.fori_loop(0, 4, body, 0, unroll=True)
+            r = (both(rhs_s, a) - out).reshape(8, 8, 256) * inside[None]
+            lv[(a - TOP) // 2] = halves(r.reshape(64, 256))
+
+        apply_rows(source, first, pairs, consume)
 
     def first_body(k, carry):
         a = TOP + 2 * k
@@ -225,8 +228,9 @@
     for d in range(5):
         cplane[d, 0:4, 0:48] = ctypes_ref[d].astype(F32)
         cplane[5 + d, 0:4, 0:48] = cscales_ref[d]
-        ft[d] = split_table(ftab_ref[d].reshape(256, 64))
-        ct[d] = split_table(ctab_ref[d].reshape(256, 64))
+        place = 256 * (0, 4, 3, 1, 2)[d]
+        ft[place:place + 256] = split_table(ftab_ref[d].reshape(256, 64))
+        ct[place:place + 256] = split_table(ctab_ref[d].reshape(256, 64))
     cs[...] = split_table(csm_ref[...].reshape(256, 64))
     g = fgroups_ref[...]
     step = lambda k: (g >= 48 * k).astype(jnp.int32)
@@ -271,14 +275,17 @@
     pack_mcol[1] = last
     pack_columns(rhs_s, 0, pack_rhs)
 
-    for copy in e0:
+    for copy in e0[2:]:
         copy.wait_recv()
-    put(xa, TOP - 1, keep(has_up, e0_row[0]))
-    put(xa, TOP + 8, keep(has_down, e0_row[1]))
     from_left = unfold(keep(has_left, e0_col[0]))
     from_right = unfold(keep(has_right, e0_col[1]))
     for i in range(8):
         put(xa, TOP + i, with_columns(st[TOP + i], from_left, from_right, i))
+    level_rows(xa, TOP + 2, 2)
+    for copy in e0[:2]:
+        copy.wait_recv()
+    put(xa, TOP - 1, keep(has_up, e0_row[0]))
+    put(xa, TOP + 8, keep(has_down, e0_row[1]))
     for k, hop in enumerate((2, -2)):
         pl.semaphore_signal(dis.at[0], inc=1, device_id=(gx, lax.rem(gy + ngy + hop, ngy)), device_id_type=MESH)
 
@@ -296,11 +303,12 @@
 
     def coarse_apply(c0, c1, top, bottom):
         here, before, after = coarse_operands(c0, c1, top, bottom)
-        out = pick(dot(ct[0], here), ctb[0], csb[0])
-        out = out + pick(dot(ct[1], before), ctb[1], csb[1])
-        out = out + pick(dot(ct[2], after), ctb[2], csb[2])
+        y = dot(ct[0:768], here)
+        out = pick(y[0:256], ctb[0], csb[0])
+        out = out + pick(dot(ct[1024:1280], before), ctb[1], csb[1])
+        out = out + pick(dot(ct[768:1024], after), ctb[2], csb[2])
         for d, shift in ((3, 1), (4, -1)):
-            part = pick(dot(ct[d], here), ctb[d], csb[d])
+            part = pick(y[256 * (d - 2):256 * (d - 1)], ctb[d], csb[d])
             out = out + jnp.concatenate([roll(part[:, :128], shift), roll(part[:, 128:], shift)], axis=-1)
         return out
 
@@ -512,7 +520,7 @@
             block = spread[:, 128 * i:128 * i + 128].reshape(8, 8, 128) * fb[TOP + i][None]
             st[TOP + i] = st[TOP + i] + block.reshape(64, 128)
 
-    def exchange(width, row_buf, col_buf, ssem, rsem, slot):
+    def exchange(width, row_buf, col_buf, ssem, rsem, slot, middle):
         pack_columns(st, slot, pack_st)
         copies = []
         n = 2
@@ -525,47 +533,56 @@
         for side, to in ((0, left), (1, right)):
             copies.append(send(pack_st.at[slot + side], col_buf.at[0, side], ssem.at[n], rsem.at[n], to))
             n += 1
-        for copy in copies:
+        far, near = copies[:-2], copies[-2:]
+
+        def columns(k):
+            return [unfold(keep(flag, col_buf[k, side])) for side, flag in ((0, has_right), (1, has_left))]
+
+        for copy in near:
             copy.wait()
-        cols = [
-            [unfold(keep(flag, col_buf[k, side])) for side, flag in ((0, has_right), (1, has_left))] for k in range(3)
-        ]
-        for a in range(TOP - width, TOP + 8 + width):
-            if a < 3:
-                block, source, i, flag = row_buf[0, a - (TOP - width)], 2, a + 5, has_up
-            elif a < 11:
-                block, source, i, flag = st[a], 0, a - 3, None
-            else:
-                block, source, i, flag = row_buf[1, a - 11], 1, a - 11, has_down
-            block = with_columns(block, cols[source][1], cols[source][0], i)
-            if flag is not None:
-                block = keep(flag, block)
+        for copy in far:
+            copy.wait_send()
+        beside = columns(0)
+        for i in range(8):
+            block = with_columns(st[TOP + i], beside[1], beside[0], i)
+            st[TOP + i] = block
+            put(xa, TOP + i, block)
+        middle()
+        for copy in far:
+            copy.wait_recv()
+        above, below = columns(2), columns(1)
+        for n in range(width):
+            a = TOP - width + n
+            block = keep(has_up, with_columns(row_buf[0, n], above[1], above[0], a + 5))
             st[a] = block
             put(xa, a, block)
-
-    level_rows(xa)
+            block = keep(has_down, with_columns(row_buf[1, n], below[1], below[0], n))
+            st[TOP + 8 + n] = block
+            put(xa, TOP + 8 + n, block)
+
+    level_rows(xa, TOP, 1)
+    level_rows(xa, TOP + 6, 1)
     for copy in e0:
         copy.wait_send()
     correct(0)
-    exchange(3, e3_row, e3_col, s3, r3, 2)
-    smooth_rows(xa, xb, 1, 6)
+    exchange(3, e3_row, e3_col, s3, r3, 2, lambda: smooth_rows(xa, xb, 5, 2))
+    smooth_rows(xa, xb, 1, 2)
+    smooth_rows(xa, xb, 9, 2)
     smooth_rows(xb, xa, 2, 5)
-    level_rows(xa)
+    level_rows(xa, TOP, 4)
     correct(1)
-    exchange(2, e6_row, e6_col, s6, r6, 4)
-    smooth_rows(xa, xb, 2, 5)
-
-    def final_body(k, carry):
-        a = TOP + 2 * k
+    exchange(2, e6_row, e6_col, s6, r6, 4, lambda: smooth_rows(xa, xb, 4, 3))
+    smooth_rows(xa, xb, 2, 1)
+    smooth_rows(xa, xb, 10, 1)
+
+    def final_pair(a, out):
         inside = jnp.concatenate([fb[a], fb[a + 1]], axis=-1)
-        r = (both(rhs_s, a) - apply_pair(xb, a)).reshape(8, 8, 256) * inside[None]
-        r = r.reshape(64, 256)
+        r = ((both(rhs_s, a) - out).reshape(8, 8, 256) * inside[None]).reshape(64, 256)
         for n in range(2):
-            res_ref[2 * k + n] = r[:, 128 * n:128 * n + 96]
-            sol_ref[2 * k + n] = st[a + n][:, 0:96]
-        return carry
-
-    lax.fori_loop(0, 4, final_body, 0, unroll=True)
+            res_ref[a - TOP + n] = r[:, 128 * n:128 * n + 96]
+            sol_ref[a - TOP + n] = st[a + n][:, 0:96]
+
+    apply_rows(xb, TOP, 4, final_pair)
 
     for copy in e1_sent:
         copy.wait_send()
@@ -616,9 +633,9 @@
                 pltpu.VMEM((5, 8, 256), F32),
                 pltpu.VMEM((5, 8, 256), F32),
                 pltpu.VMEM((8, 256), F32),
-                pltpu.VMEM((5, 256, 256), BF16),
+                pltpu.VMEM((1280, 256), BF16),
                 pltpu.VMEM((256, 256), BF16),
-                pltpu.VMEM((5, 256, 256), BF16),
+                pltpu.VMEM((1280, 256), BF16),
                 pltpu.VMEM((256, 256), BF16),
                 pltpu.VMEM((256, 1024), BF16),
                 pltpu.VMEM((4, 128, 256), BF16),

time: 74.6 us -> 70.2 us (0.941)
  Pallas kernels: 72.4 us -> 68 us
    pallas_call x1, Pallas kernels: 72.4 us -> 68 us  [shards(): pl.pallas_call(functools.partial(kernel, ngx, ngy), out_shape=(pltpu.VMEM...]
where the time goes in v2:
time: 70.2 us; the launch traced here: 70.1 us
  Pallas kernels  68 us (97%)
  local copies, waits for them, and re-layouts  1.41 us (2%)
    pallas_call x1, Pallas kernels, shards(): pl.pallas_call(functools.partial(kernel, ngx, ngy), out_shape=(pltpu.VMEM...  68 us
    unnamed x2, local copies, waits for them, and re-layouts  1.41 us

profile of v2, /device:TPU:1, one launch (start us, length us, event | category | flops | bytes accessed | tf_op | source)
XLA Modules:
  0.0 70.1 jit_solution(5165632629096269191)
XLA Ops:
  0.6 68.0 %shard_map.140 = (f32[8,64,96]{2,1,0:T(8,128)S(1)}, f32[8,64,96]{2,1,0:T(8,128)S(1)}) custom-call(f32[8,64,96]{2,1,0:T(8,128)} %bitcast.5, s32[8,96]{1,0:T(8,128)} %active_in.1, s32[5,8,96]{2,1,0:T(8,128)} %ftypes_in.1, f32[5,8,96]{2,1,0:T(8,128)} %fscales_in.1, f32[5,4,64,64]{3,2,1,0:T(8,128)} %ftab_in.1, f32[4,64,64]{2,1,0:T(8,128)} %fsm_in.1, ...), custom_call_target="tpu_custom_call" | custom-call | tf_op jit(solution)/shard_map/pallas_call | solution.py:604
  68.6 0.7 %copy.17 = f32[8,96,64]{1,2,0:T(8,128)} copy(f32[8,96,64]{1,2,0:T(8,128)S(1)} %bitcast.4) | data formatting | bytes 393216
  69.3 0.7 %copy.18 = f32[8,96,64]{1,2,0:T(8,128)} copy(f32[8,96,64]{1,2,0:T(8,128)S(1)} %bitcast.3) | data formatting | bytes 393216
